TPU v7x, 256 devices: a whole 4x4x8 slice. The times are simulated.
256 devices in a mesh: sub: 16 (over y, x), grp: 16 (over z, core).
Axes of the slice: x: 4, y: 4, z: 8, core: 2. Of those that a mesh axis runs over, the one named last changes fastest.
Arguments:
- applied_loads: float32 [16, 16, 64, 1536], P('sub', 'grp')
- flex_matrix: bfloat16 [16, 16, 1536, 1536], P('sub', 'grp'), as said below
- schur_matrix: bfloat16 [16, 16, 1536, 1536], P('sub', 'grp'), as said below
- corner_coupling: float32 [16, 16, 12, 1536], P('sub', 'grp'), may hold values from -0.625 to 0.625
- coarse_inverse: float32 [768, 768], replicated, as said below
- face_match: int32 [16, 16, 4, 384], P('sub', 'grp'), may hold values from 0 to 383, as said below
- corner_map: int32 [16, 16, 12], P('sub', 'grp'), may hold values from 0 to 767, as said below
Outputs:
- multipliers: float32 [16, 16, 64, 4, 384], P('sub', 'grp')
- residual: float32 [16, 16, 64, 4, 384], P('sub', 'grp')
Inputs may be any that keep to these rules, and one draw needn't show every extreme that they name: `flex_matrix`: each subdomain's matrix is symmetric positive definite. `schur_matrix`: each subdomain's matrix is symmetric positive definite. `coarse_inverse`: lower triangular with a positive diagonal. face_match[s, g, 1] is a permutation of the 384 face nodes and face_match[s+1, g, 0] is its inverse; face_match[s, g, 3] and face_match[s, g+1, 2] likewise (indices wrap). `corner_map`: the 12 entries of one subdomain are distinct; every corner unknown is named by exactly four subdomains.
All inputs are finite; a program needn't handle non-finite values.
Results may differ from a plain program's by a relative error of at most 0.0088.
Values sent between devices are 32-bit elements; how exact they have to be, the bound alone decides.
A program may use at most 64 MiB of HBM per device.

v0:
```python
import jax
import jax.numpy as jnp
from jax import lax
from jax.sharding import PartitionSpec as P

ITERS = 2


def extended(x, sides, width):
    for axis, dim in sides:
        peers, length = (lax.axis_size(axis), x.shape[dim])
        up = [(i, (i + 1) % peers) for i in range(peers)]
        down = [(j, i) for i, j in up]
        last = lax.slice_in_dim(x, length - width, length, axis=dim)
        first = lax.slice_in_dim(x, 0, width, axis=dim)
        before = lax.ppermute(last, axis, up)
        after = lax.ppermute(first, axis, down)
        x = jnp.concatenate([before, x, after], axis=dim)
    return x


def shards(
    applied_loads,
    flex_matrix,
    schur_matrix,
    corner_coupling,
    coarse_inverse,
    face_match,
    corner_map,
):
    highest = lax.Precision.HIGHEST
    load_cases = applied_loads.shape[2]
    interface = applied_loads.shape[3]
    face_size = interface // 4
    flex_local = flex_matrix[0, 0]
    schur_local = schur_matrix[0, 0]
    coupling_local = corner_coupling[0, 0]
    matching = face_match[0, 0]
    corners = corner_map[0, 0]
    coarse_size = coarse_inverse.shape[0]
    selector = (corners[:, None] == jnp.arange(coarse_size, dtype=jnp.int32)[None, :]).astype(
        jnp.float32
    )
    face_signs = jnp.array([-1.0, 1.0, -1.0, 1.0], jnp.float32)[:, None]
    contract_last = (((1,), (1,)), ((), ()))

    def neighbour_jump(displaced):
        around_sub = extended(displaced[:, 0:2], (("sub", 1),), 1)
        around_grp = extended(displaced[:, 2:4], (("grp", 1),), 1)
        from_left_sub = jnp.take(around_sub[:, 0], matching[0], axis=1)
        from_right_sub = jnp.take(around_sub[:, 3], matching[1], axis=1)
        from_left_grp = jnp.take(around_grp[:, 0], matching[2], axis=1)
        from_right_grp = jnp.take(around_grp[:, 3], matching[3], axis=1)
        return jnp.stack(
            [
                from_left_sub - displaced[:, 0],
                displaced[:, 1] - from_right_sub,
                from_left_grp - displaced[:, 2],
                displaced[:, 3] - from_right_grp,
            ],
            axis=1,
        )

    def apply_precond(current):
        weighted = (0.5 * current * face_signs).reshape(load_cases, interface).astype(jnp.bfloat16)
        response = jnp.dot(weighted, schur_local, preferred_element_type=jnp.float32)
        return 0.5 * neighbour_jump(response.reshape(load_cases, 4, face_size))

    def inner(former, latter):
        return lax.psum(0.5 * jnp.sum(former * latter, axis=(1, 2)), ("sub", "grp"))

    right_side = neighbour_jump(applied_loads[0, 0].reshape(load_cases, 4, face_size))
    multipliers = jnp.zeros(right_side.shape, jnp.float32)
    residual = right_side
    precond = apply_precond(residual)
    precond_dot = inner(residual, precond)
    direction = precond
    for iteration in range(ITERS):
        forces = (direction * face_signs).reshape(load_cases, interface)
        apply_free = jnp.dot(
            forces.astype(jnp.bfloat16), flex_local, preferred_element_type=jnp.float32
        )
        corner = lax.dot_general(forces, coupling_local, contract_last, precision=highest)
        share = jnp.dot(corner, selector, precision=highest)
        apply_coarse_total = lax.psum(share, ("sub", "grp"))
        lowered = lax.dot_general(
            apply_coarse_total, coarse_inverse, contract_last, precision=highest
        )
        picked = lax.dot_general(
            jnp.dot(lowered, coarse_inverse, precision=highest),
            selector,
            contract_last,
            precision=highest,
        )
        apply_displaced = apply_free + jnp.dot(picked, coupling_local, precision=highest)
        curvature = lax.psum(jnp.sum(forces * apply_displaced, axis=1), ("sub", "grp"))
        image, curvature = (
            neighbour_jump(apply_displaced.reshape(load_cases, 4, face_size)),
            curvature,
        )
        step_size = (precond_dot / curvature)[:, None, None]
        multipliers = multipliers + step_size * direction
        residual = residual - step_size * image
        if iteration + 1 < ITERS:
            precond = apply_precond(residual)
            next_dot = inner(residual, precond)
            direction = precond + (next_dot / precond_dot)[:, None, None] * direction
            precond_dot = next_dot
    return (multipliers[None, None], residual[None, None])


def solution(mesh):
    return jax.shard_map(
        shards,
        mesh=mesh,
        in_specs=(
            P("sub", "grp", None, None),
            P("sub", "grp", None, None),
            P("sub", "grp", None, None),
            P("sub", "grp", None, None),
            P(),
            P("sub", "grp", None, None),
            P("sub", "grp", None),
        ),
        out_specs=(P("sub", "grp", None, None, None), P("sub", "grp", None, None, None)),
        check_vma=False,
    )
```

profile of v0, /device:TPU:1, one launch (start us, length us, event | category | flops | bytes accessed | tf_op | source)
XLA Modules:
  0.0 913.4 jit_solution(17295880697463519003)
XLA Ops:
  8.8 2.1 collective-permute-start
  10.9 3.8 collective-permute-start.1
  15.4 2.6 collective-permute-start.2
  19.2 6.6 copy.118
  39.3 4.0 fusion.81
  45.4 2.0 collective-permute-start.6
  50.7 1.6 gather_fusion.5
  52.3 1.7 copy.71
  55.1 1.6 gather_fusion.6
  56.7 1.7 copy.73
  59.4 1.6 gather_fusion.7
  61.0 1.7 copy.75
  63.7 1.6 gather_fusion.4
  66.4 1.8 fusion.45
  70.8 1.6 fusion.35
  73.9 1.6 copy.133
  75.5 246.2 %all-reduce.4.cloned.1.call-done = f32[64,768]{1,0:T(8,128)} async-done(((f32[64,768]{1,0:T(8,128)}), f32[64,768]{1,0:T(8,128)}) %all-reduce.4.cloned.1.call-update) | async-done | bytes 196624 | tf_op jit(solution)/shard_map/psum | solution.py:85
  321.7 3.3 fusion.82
  328.0 4.0 multiply_reduce_fusion.2
  332.8 1.9 fusion.78
  336.8 3.5 collective-permute-start.9
  342.8 74.8 %all-reduce = (f32[64]{0:T(128)}, f32[64]{0:T(128)}) all-reduce(f32[64]{0:T(128)} %broadcast_multiply_fusion.2, f32[64]{0:T(128)} %get-tuple-element.88), channel_id=1, replica_groups=mesh['sub'=16,'grp'=16] {'sub','grp'}, use_global_device_ids=true, to_apply=%region_1.3 | all-reduce | flops 128 | bytes 1024 | tf_op jit(solution)/shard_map/psum | solution.py:70
  420.5 1.6 gather_fusion.8
  423.2 1.6 fusion.52
  425.8 1.6 gather_fusion.9
  428.5 1.6 fusion.54
  431.1 1.6 gather_fusion.10
  433.8 1.6 fusion.56
  436.4 1.6 gather_fusion.11
  440.7 1.9 multiply_convert_fusion
  442.8 3.9 fusion.84
  449.2 2.0 collective-permute-start.14
  453.7 1.6 gather_fusion.15
  455.3 1.7 copy.100
  458.0 1.6 gather_fusion.13
  459.7 1.7 copy.96
  462.4 1.6 gather_fusion.14
  464.0 1.7 copy.98
  466.7 1.6 gather_fusion.12
  468.3 1.7 copy.94
  470.0 1.9 fusion.61
  474.2 76.3 %psum.45 = f32[64]{0:T(128)} all-reduce(f32[64]{0:T(128)} %broadcast_multiply_fusion), channel_id=1, replica_groups=mesh['sub'=16,'grp'=16] {'sub','grp'}, use_global_device_ids=true, to_apply=%region_6.8 | all-reduce | flops 64 | bytes 512 | tf_op jit(solution)/shard_map/psum | solution.py:70
  551.2 1.9 convert_bitcast_fusion
  557.1 239.5 %all-reduce.6.cloned.1.call-done = f32[64,768]{1,0:T(8,128)} async-done(((f32[64,768]{1,0:T(8,128)}), f32[64,768]{1,0:T(8,128)}) %all-reduce.6.cloned.1.call-update) | async-done | bytes 196624 | tf_op jit(solution)/shard_map/psum | solution.py:85
  796.6 3.3 fusion.85
  802.2 4.7 multiply_reduce_fusion
  810.9 3.5 collective-permute-start.17
  816.9 75.1 %psum.47 = f32[64]{0:T(128)S(1)} all-reduce(f32[64]{0:T(128)} %get-tuple-element.90), channel_id=1, replica_groups=mesh['sub'=16,'grp'=16] {'sub','grp'}, use_global_device_ids=true, to_apply=%region_9.11 | all-reduce | flops 64 | bytes 512 | tf_op jit(solution)/shard_map/psum | solution.py:96
  (214 shorter events, 88.8 us)
Async XLA Ops:
  7.2 314.5 %copy-start = (f32[768,768]{1,0:T(8,128)S(1)}, f32[768,768]{1,0:T(8,128)}, u32[]{:S(2)}) copy-start(f32[768,768]{1,0:T(8,128)} %param.14) | copy-start | bytes 7077892
  7.2 314.5 %all-reduce.4.cloned.1.call-start = ((), (), s32[]{:S(2)}) async-start(), calls=%async_computation | async-start | bytes 393216 | tf_op jit(solution)/shard_map/psum | solution.py:85
  8.8 17.0 %collective-permute-start = (f32[64,1,384]{2,0,1:T(8,128)S(1)}, f32[64,1,384]{2,0,1:T(8,128)S(1)}, u32[]{:S(2)}, u32[]{:S(2)}) collective-permute-start(f32[64,1,384]{2,0,1:T(8,128)S(1)} %copy.120), channel_id=1, source_target_pairs={{0,16},{16,32},{32,48},{48,64},{64,80},{80,96},{96,112},{112,128},... | collective-permute-start | bytes 294920 | tf_op jit(solution)/shard_map/ppermute | solution.py:16
  10.9 16.3 %collective-permute-start.1 = (f32[64,1,384]{2,0,1:T(8,128)S(1)}, f32[64,1,384]{2,0,1:T(8,128)}, u32[]{:S(2)}, u32[]{:S(2)}) collective-permute-start(f32[64,1,384]{2,0,1:T(8,128)S(1)} %copy.121), channel_id=1, source_target_pairs={{16,0},{32,16},{48,32},{64,48},{80,64},{96,80},{112,96},{128,112},... | collective-permute-start | bytes 294920 | tf_op jit(solution)/shard_map/ppermute | solution.py:17
  15.4 14.1 %collective-permute-start.2 = (f32[64,1,384]{2,0,1:T(8,128)}, f32[64,1,384]{2,0,1:T(8,128)}, u32[]{:S(2)}, u32[]{:S(2)}) collective-permute-start(f32[64,1,384]{2,0,1:T(8,128)} %copy.122), channel_id=1, source_target_pairs={{0,1},{1,2},{2,3},{3,4},{4,5},{5,6},{6,7},{7,8},{8,9},{9,10},{10,1... | collective-permute-start | bytes 294920 | tf_op jit(solution)/shard_map/ppermute | solution.py:16
  18.0 14.4 %collective-permute-start.3 = (f32[64,1,384]{2,0,1:T(8,128)S(1)}, f32[64,1,384]{2,0,1:T(8,128)}, u32[]{:S(2)}, u32[]{:S(2)}) collective-permute-start(f32[64,1,384]{2,0,1:T(8,128)S(1)} %copy.123), channel_id=1, source_target_pairs={{1,0},{2,1},{3,2},{4,3},{5,4},{6,5},{7,6},{8,7},{9,8},{10,9},{11,1... | collective-permute-start | bytes 294920 | tf_op jit(solution)/shard_map/ppermute | solution.py:17
  25.8 12.5 %copy-start.23 = (f32[4]{0:T(128)S(1)}, f32[4]{0:T(128)}, u32[]{:S(2)}) copy-start(f32[4]{0:T(128)} %constant.24) | copy-start | bytes 52
  37.6 30.6 %copy-start.5 = (f32[64,1,384]{2,0,1:T(8,128)}, f32[64,1,384]{2,0,1:T(8,128)S(1)}, u32[]{:S(2)}) copy-start(f32[64,1,384]{2,0,1:T(8,128)S(1)} %get-tuple-element.85) | copy-start | bytes 294916
  38.3 29.9 %copy-start.7 = (f32[64,1,384]{2,0,1:T(8,128)}, f32[64,1,384]{2,0,1:T(8,128)S(1)}, u32[]{:S(2)}) copy-start(f32[64,1,384]{2,0,1:T(8,128)S(1)} %get-tuple-element.87) | copy-start | bytes 294916
  44.0 5.0 collective-permute-start.5
  45.4 8.6 collective-permute-start.6
  47.4 10.9 %collective-permute-start.7 = (f32[64,1,384]{2,0,1:T(8,128)}, f32[64,1,384]{2,0,1:T(8,128)}, u32[]{:S(2)}, u32[]{:S(2)}) collective-permute-start(f32[64,1,384]{2,0,1:T(8,128)} %get-tuple-element.65), channel_id=1, source_target_pairs={{1,0},{2,1},{3,2},{4,3},{5,4},{6,5},{7,6},{8,7},{9,8},{10,9},{11,1... | collective-permute-start | bytes 294920 | tf_op jit(solution)/shard_map/ppermute | solution.py:17
  48.9 13.8 %collective-permute-start.4 = (f32[64,1,384]{2,0,1:T(8,128)S(1)}, f32[64,1,384]{2,0,1:T(8,128)}, u32[]{:S(2)}, u32[]{:S(2)}) collective-permute-start(f32[64,1,384]{2,0,1:T(8,128)S(1)} %get-tuple-element.64), channel_id=1, source_target_pairs={{0,16},{16,32},{32,48},{48,64},{64,80},{80,96},{96,112},{112,128},... | collective-permute-start | bytes 294920 | tf_op jit(solution)/shard_map/ppermute | solution.py:16
  52.3 18.0 %copy-start.1 = (f32[1,1,12,1536]{3,1,2,0:T(1,128)S(1)}, f32[1,1,12,1536]{3,1,2,0:T(1,128)}, u32[]{:S(2)}) copy-start(f32[1,1,12,1536]{3,1,2,0:T(1,128)} %param.13) | copy-start | bytes 221188
  68.2 2.7 copy-start.2
  68.2 2.7 copy-start.3
  68.2 2.7 copy-start.4
  72.5 724.1 %all-reduce.6.cloned.1.call-start = ((), (), s32[]{:S(2)}) async-start(), calls=%async_computation.1 | async-start | bytes 393216 | tf_op jit(solution)/shard_map/psum | solution.py:85
  321.7 6.3 copy-start.16
  332.8 107.8 %copy-start.6 = (f32[64,1,384]{2,0,1:T(8,128)S(1)}, f32[64,1,384]{2,0,1:T(8,128)}, u32[]{:S(2)}) copy-start(f32[64,1,384]{2,0,1:T(8,128)} %copy-done.5) | copy-start | bytes 294916
  332.8 107.8 %copy-start.8 = (f32[64,1,384]{2,0,1:T(8,128)S(1)}, f32[64,1,384]{2,0,1:T(8,128)}, u32[]{:S(2)}) copy-start(f32[64,1,384]{2,0,1:T(8,128)} %copy-done.7) | copy-start | bytes 294916
  332.8 107.8 %copy-start.24 = (f32[4]{0:T(128)S(1)}, f32[4]{0:T(128)}, u32[]{:S(2)}) copy-start(f32[4]{0:T(128)} %constant.24) | copy-start | bytes 52
  334.7 5.6 copy-start.12
  334.7 7.4 copy-start.13
  334.8 8.0 copy-start.14
  334.8 8.0 copy-start.15
  334.8 84.1 %collective-permute-start.8 = (f32[64,1,384]{2,0,1:T(8,128)S(1)}, f32[64,1,384]{2,0,1:T(8,128)S(1)}, u32[]{:S(2)}, u32[]{:S(2)}) collective-permute-start(f32[64,1,384]{2,0,1:T(8,128)S(1)} %copy.124), channel_id=1, source_target_pairs={{0,16},{16,32},{32,48},{48,64},{64,80},{80,96},{96,112},{112,128},... | collective-permute-start | bytes 294920 | tf_op jit(solution)/shard_map/ppermute | solution.py:16
  336.8 88.0 %collective-permute-start.9 = (f32[64,1,384]{2,0,1:T(8,128)}, f32[64,1,384]{2,0,1:T(8,128)}, u32[]{:S(2)}, u32[]{:S(2)}) collective-permute-start(f32[64,1,384]{2,0,1:T(8,128)} %copy.125), channel_id=1, source_target_pairs={{16,0},{32,16},{48,32},{64,48},{80,64},{96,80},{112,96},{128,112},... | collective-permute-start | bytes 294920 | tf_op jit(solution)/shard_map/ppermute | solution.py:17
  341.0 89.1 %collective-permute-start.10 = (f32[64,1,384]{2,0,1:T(8,128)}, f32[64,1,384]{2,0,1:T(8,128)}, u32[]{:S(2)}, u32[]{:S(2)}) collective-permute-start(f32[64,1,384]{2,0,1:T(8,128)} %copy.126), channel_id=1, source_target_pairs={{0,1},{1,2},{2,3},{3,4},{4,5},{5,6},{6,7},{7,8},{8,9},{9,10},{10,1... | collective-permute-start | bytes 294920 | tf_op jit(solution)/shard_map/ppermute | solution.py:16
  342.8 92.6 %collective-permute-start.11 = (f32[64,1,384]{2,0,1:T(8,128)}, f32[64,1,384]{2,0,1:T(8,128)}, u32[]{:S(2)}, u32[]{:S(2)}) collective-permute-start(f32[64,1,384]{2,0,1:T(8,128)} %copy.127), channel_id=1, source_target_pairs={{1,0},{2,1},{3,2},{4,3},{5,4},{6,5},{7,6},{8,7},{9,8},{10,9},{11,1... | collective-permute-start | bytes 294920 | tf_op jit(solution)/shard_map/ppermute | solution.py:17
  418.8 135.8 %copy-start.27 = (f32[64]{0:T(128)}, f32[64]{0:T(128)S(1)}, u32[]{:S(2)}) copy-start(f32[64]{0:T(128)S(1)} %get-tuple-element.14) | copy-start | bytes 772
  447.4 4.6 collective-permute-start.15
  448.1 8.9 collective-permute-start.13
  449.2 12.1 %collective-permute-start.14 = (f32[64,1,384]{2,0,1:T(8,128)}, f32[64,1,384]{2,0,1:T(8,128)}, u32[]{:S(2)}, u32[]{:S(2)}) collective-permute-start(f32[64,1,384]{2,0,1:T(8,128)} %get-tuple-element.57), channel_id=1, source_target_pairs={{0,1},{1,2},{2,3},{3,4},{4,5},{5,6},{6,7},{7,8},{8,9},{9,10},{10,1... | collective-permute-start | bytes 294920 | tf_op jit(solution)/shard_map/ppermute | solution.py:16
  451.2 14.5 %collective-permute-start.12 = (f32[64,1,384]{2,0,1:T(8,128)}, f32[64,1,384]{2,0,1:T(8,128)}, u32[]{:S(2)}, u32[]{:S(2)}) collective-permute-start(f32[64,1,384]{2,0,1:T(8,128)} %get-tuple-element.55), channel_id=1, source_target_pairs={{0,16},{16,32},{32,48},{48,64},{64,80},{80,96},{96,112},{112,128},... | collective-permute-start | bytes 294920 | tf_op jit(solution)/shard_map/ppermute | solution.py:16
  458.0 95.6 %copy-start.25 = (s32[1,1,12]{2,1,0:T(1,128)S(1)}, s32[1,1,12]{2,1,0:T(1,128)}, u32[]{:S(2)}) copy-start(s32[1,1,12]{2,1,0:T(1,128)} %param.16) | copy-start | bytes 148
  551.2 2.4 copy-start.29
  553.1 248.3 %copy-start.26 = (s32[1,1,12]{2,1,0:T(1,128)S(1)}, s32[1,1,12]{2,1,0:T(1,128)}, u32[]{:S(2)}) copy-start(s32[1,1,12]{2,1,0:T(1,128)} %param.16) | copy-start | bytes 148
  557.1 245.1 %copy-start.9 = (f32[4,8,8,384]{3,2,0,1:T(8,128)S(1)}, f32[4,8,8,384]{3,2,0,1:T(8,128)}, u32[]{:S(2)}) copy-start(f32[4,8,8,384]{3,2,0,1:T(8,128)} %copy.135) | copy-start | bytes 1179652
  796.6 5.6 copy-start.30
  801.7 90.9 %copy-start.17 = (f32[1,1,64,1,384]{4,2,3,1,0:T(8,128)S(1)}, f32[1,1,64,1,384]{4,2,3,1,0:T(8,128)}, u32[]{:S(2)}) copy-start(f32[1,1,64,1,384]{4,2,3,1,0:T(8,128)} %get-tuple-element.27) | copy-start | bytes 294916
  809.0 86.0 %collective-permute-start.16 = (f32[64,1,384]{2,0,1:T(8,128)}, f32[64,1,384]{2,0,1:T(8,128)}, u32[]{:S(2)}, u32[]{:S(2)}) collective-permute-start(f32[64,1,384]{2,0,1:T(8,128)} %copy.128), channel_id=1, source_target_pairs={{0,16},{16,32},{32,48},{48,64},{64,80},{80,96},{96,112},{112,128},... | collective-permute-start | bytes 294920 | tf_op jit(solution)/shard_map/ppermute | solution.py:16
  810.9 86.4 %collective-permute-start.17 = (f32[64,1,384]{2,0,1:T(8,128)}, f32[64,1,384]{2,0,1:T(8,128)}, u32[]{:S(2)}, u32[]{:S(2)}) collective-permute-start(f32[64,1,384]{2,0,1:T(8,128)} %copy.129), channel_id=1, source_target_pairs={{16,0},{32,16},{48,32},{64,48},{80,64},{96,80},{112,96},{128,112},... | collective-permute-start | bytes 294920 | tf_op jit(solution)/shard_map/ppermute | solution.py:17
  814.4 89.8 %copy-start.18 = (f32[1,1,64,1,384]{4,2,3,1,0:T(8,128)S(1)}, f32[1,1,64,1,384]{4,2,3,1,0:T(8,128)}, u32[]{:S(2)}) copy-start(f32[1,1,64,1,384]{4,2,3,1,0:T(8,128)} %get-tuple-element.80) | copy-start | bytes 294916
  814.4 89.8 %copy-start.19 = (f32[1,1,64,1,384]{4,2,3,1,0:T(8,128)S(1)}, f32[1,1,64,1,384]{4,2,3,1,0:T(8,128)}, u32[]{:S(2)}) copy-start(f32[1,1,64,1,384]{4,2,3,1,0:T(8,128)} %get-tuple-element.82) | copy-start | bytes 294916
  814.4 89.8 %copy-start.28 = (f32[64]{0:T(128)S(1)}, f32[64]{0:T(128)}, u32[]{:S(2)}) copy-start(f32[64]{0:T(128)} %copy-done.27) | copy-start | bytes 772
  815.1 84.5 %collective-permute-start.18 = (f32[64,1,384]{2,0,1:T(8,128)}, f32[64,1,384]{2,0,1:T(8,128)}, u32[]{:S(2)}, u32[]{:S(2)}) collective-permute-start(f32[64,1,384]{2,0,1:T(8,128)} %copy.130), channel_id=1, source_target_pairs={{0,1},{1,2},{2,3},{3,4},{4,5},{5,6},{6,7},{7,8},{8,9},{9,10},{10,1... | collective-permute-start | bytes 294920 | tf_op jit(solution)/shard_map/ppermute | solution.py:16
  816.9 85.0 %collective-permute-start.19 = (f32[64,1,384]{2,0,1:T(8,128)}, f32[64,1,384]{2,0,1:T(8,128)}, u32[]{:S(2)}, u32[]{:S(2)}) collective-permute-start(f32[64,1,384]{2,0,1:T(8,128)} %copy.131), channel_id=1, source_target_pairs={{1,0},{2,1},{3,2},{4,3},{5,4},{6,5},{7,6},{8,7},{9,8},{10,9},{11,1... | collective-permute-start | bytes 294920 | tf_op jit(solution)/shard_map/ppermute | solution.py:17
  (5 other events, 4.4 us)
Sparse Core Ops, SparseCore 0:
  72.6 249.0 all-reduce.3
  554.7 241.7 all-reduce.5
where the time goes:
time: 915 us; the launch traced here: 913 us
  waiting for transfers between devices  486 us (53%)
  blocking collectives  226 us (25%)
  local copies, waits for them, and re-layouts  96.5 us (11%)
  matrix products  31.8 us (3%)
  starting transfers between devices  30 us (3%)
  other arithmetic  27.9 us (3%)
  between operations  14.7 us (2%)
    psum x2, waiting for transfers between devices, shards(): apply_coarse_total = lax.psum(share, ('sub', 'grp'))  486 us
    psum x2, blocking collectives, inner(): return lax.psum(0.5 * jnp.sum(former * latter, axis=(1, 2)), ('sub', 'grp'))  151 us
    psum x1, blocking collectives, shards(): lax.psum(jnp.sum(forces * apply_displaced, axis=1), ('sub', 'grp'))  75.1 us
  transfers between devices with their start and end apart: 22, of which 3 were waited for; matrix products, arithmetic and copies ran while one was open for 8% of the time, Pallas kernels for 0%

commit v1 on v0

v1 whole, which is shorter than its diff:
```python
import functools

import jax
import jax.numpy as jnp
from jax import lax
from jax.experimental import pallas as pl
from jax.experimental.pallas import tpu as pltpu
from jax.sharding import PartitionSpec as P

MESH = pl.DeviceIdType.MESH
F32 = jnp.float32
BF16 = jnp.bfloat16
OPPOSITE = (1, 0, 3, 2)
ANY = pl.BlockSpec(memory_space=pl.ANY)
VMEM = pl.BlockSpec(memory_space=pltpu.VMEM)
NT = (((1,), (1,)), ((), ()))


def dot(a, b):
    return jnp.dot(a, b, preferred_element_type=F32)


def dot_nt(a, b):
    return lax.dot_general(a, b, NT, preferred_element_type=F32)


def split(x):
    high = x.astype(BF16)
    return high, (x - high.astype(F32)).astype(BF16)


def stacked(x):
    return jnp.concatenate(split(x), axis=0)


def lane_chunks(x):
    total = x[:, 0:128]
    for c in range(1, x.shape[1] // 128):
        total = total + x[:, 128 * c : 128 * c + 128]
    return total


def kernel(
    n_sub, n_grp,
    loads_hbm, flex_hbm, schur_hbm, coupling_hbm, inverse_hbm, match_hbm, corner_hbm,
    mult_out, res_out,
    loads, flex, schur, coupling, inverse, match, corner, corner_pad,
    halo, near_coupling, near_corner,
    perm, wide_g, select, near_inverse, inv_hi, inv_lo,
    y_buf, free0, free1, res, z0, image0,
    dense, recv1, part, recv2, total, rhs,
    small, small_recv1, small2, small_recv2,
    local_sem, halo_send, halo_recv, near_send, near_recv,
    send1, rec1, send2, rec2, send3, rec3, ssend1, srec1, ssend2, srec2,
):
    s, g = lax.axis_index("sub"), lax.axis_index("grp")
    load_cases, interface = loads.shape
    face = interface // 4
    half = interface // 2
    size = inverse.shape[0]

    def sub_peer(d):
        return (lax.rem(s + d, n_sub), g)

    def grp_peer(d):
        return (s, lax.rem(g + d, n_grp))

    near = (sub_peer(n_sub - 1), sub_peer(1), grp_peer(n_grp - 1), grp_peer(1))

    def faces(f):
        return slice(face * f, face * f + face)

    def remote(src, dst, send, recv, to):
        copy = pltpu.make_async_remote_copy(
            src_ref=src, dst_ref=dst, send_sem=send, recv_sem=recv, device_id=to, device_id_type=MESH
        )
        copy.start()
        return copy

    barrier = pltpu.get_barrier_semaphore()
    for d in range(1, n_sub):
        pl.semaphore_signal(barrier, inc=1, device_id=sub_peer(d), device_id_type=MESH)
    for d in range(1, n_grp):
        pl.semaphore_signal(barrier, inc=1, device_id=grp_peer(d), device_id_type=MESH)

    sources = (
        (corner_hbm, corner), (loads_hbm.at[0, 0], loads), (match_hbm.at[0, 0], match),
        (coupling_hbm.at[0, 0], coupling), (schur_hbm.at[0, 0], schur), (inverse_hbm, inverse),
        (flex_hbm.at[0, 0], flex),
    )
    local = []
    for i, (src, dst) in enumerate(sources):
        copy = pltpu.make_async_copy(src, dst, local_sem.at[i])
        copy.start()
        local.append(copy)
    corner_copy, loads_copy, match_copy, coupling_copy, schur_copy, inverse_copy, flex_copy = local

    corner_copy.wait()
    corner_pad[...] = jnp.full(corner_pad.shape, -1, jnp.int32)
    corner_pad[0:1, 0 : corner.shape[2]] = corner[0]
    coupling_copy.wait()
    loads_copy.wait()
    pl.semaphore_wait(barrier, n_sub + n_grp - 2)

    pending = []

    def send_halo(step, f, src):
        copy = remote(
            src, halo.at[step, OPPOSITE[f]], halo_send.at[step, f], halo_recv.at[step, OPPOSITE[f]], near[f]
        )
        pending.append(copy)
        return copy

    arrivals = {}
    for f in range(4):
        arrivals[0, OPPOSITE[f]] = send_halo(0, f, loads.at[:, faces(f)])
    near_copies = []
    for f in range(4):
        o = OPPOSITE[f]
        near_copies.append(
            remote(coupling.at[:, faces(f)], near_coupling.at[o], near_send.at[0, f], near_recv.at[0, o], near[f])
        )
        near_copies.append(remote(corner_pad, near_corner.at[o], near_send.at[1, f], near_recv.at[1, o], near[f]))
    pending.extend(near_copies)

    match_copy.wait()
    row = lax.broadcasted_iota(jnp.int32, (face, face), 0)
    for f in range(4):
        perm[f] = (row == match[f : f + 1, :]).astype(BF16)

    def neighbour(step, f):
        arrivals[step, f].wait_recv()
        both = dot(stacked(halo[step, f]), perm[f])
        return both[:load_cases] + both[load_cases:]

    def send_out(step, f0, ref):
        for f in (f0, f0 + 1):
            arrivals[step, OPPOSITE[f]] = send_halo(step, f, ref.at[:, faces(f)])

    for f in range(4):
        res[:, faces(f)] = loads[:, faces(f)] - neighbour(0, f)

    def apply_schur(step):
        weighted = (0.5 * res[...]).astype(BF16)
        for h in range(2):
            cut = slice(half * h, half * h + half)
            y_buf[step // 2, :, cut] = dot(weighted, schur[:, cut])
            send_out(step, 2 * h, y_buf.at[step // 2])

    schur_copy.wait()
    apply_schur(1)

    for copy in near_copies:
        copy.wait_recv()
    wide_g[...] = jnp.zeros(wide_g.shape, BF16)
    own_hi, own_lo = split(coupling[...])
    corners = own_hi.shape[0]
    wide_g[0, 0:corners, :] = own_hi
    wide_g[1, 0:corners, :] = own_lo
    for f in range(4):
        hi, lo = split(near_coupling[f])
        wide_g[0, 16 * f + 16 : 16 * f + 16 + corners, faces(f)] = (-dot(hi, perm[f])).astype(BF16)
        wide_g[1, 16 * f + 16 : 16 * f + 16 + corners, faces(f)] = (-dot(lo, perm[f])).astype(BF16)
    lane = lax.broadcasted_iota(jnp.int32, (8, 128), 1)
    numbers = jnp.where(lane < corners, corner_pad[...], -1)
    for f in range(4):
        start = 16 * f + 16
        inside = jnp.logical_and(lane >= start, lane < start + corners)
        numbers = jnp.where(inside, pltpu.roll(near_corner[f], start, 1), numbers)
    column = jnp.broadcast_to(numbers.astype(F32)[0:1, :], (128, 128)).T
    unknown = lax.broadcasted_iota(jnp.int32, (128, size), 1).astype(F32)
    select[...] = (column[:, 0:1] == unknown).astype(BF16)

    def start_coarse(it, y):
        pair = dot_nt(stacked(0.5 * y), jnp.concatenate([wide_g[0], wide_g[1]], axis=0))
        mine = pair[:load_cases, :128] + pair[:load_cases, 128:] + pair[load_cases:, :128]
        spread = dot(stacked(mine), select[...])
        spread = spread[:load_cases] + spread[load_cases:]
        for t in range(n_sub):
            lg, h = t % 8, t // 8
            dense[it, t] = spread[8 * lg : 8 * lg + 8, size // 2 * h : size // 2 * h + size // 2]
        copies = []
        for d in range(1, n_sub):
            to = sub_peer(d)
            copies.append(
                remote(dense.at[it, to[0]], recv1.at[it, d], send1.at[it, d], rec1.at[it, d], to)
            )
        pending.extend(copies)
        return copies

    def middle_coarse(it, copies):
        acc = dense[it, s]
        for d in range(1, n_sub):
            copies[d - 1].wait_recv()
            acc = acc + recv1[it, d]
        part[it] = acc
        out = [
            remote(part.at[it], recv2.at[it, d], send2.at[it, d], rec2.at[it, d], grp_peer(d))
            for d in range(1, n_grp)
        ]
        pending.extend(out)
        return out

    def last_coarse(it, copies):
        acc = part[it]
        for d in range(1, n_grp):
            copies[d - 1].wait_recv()
            acc = acc + recv2[it, d]
        total[it] = acc
        rhs[it, s] = acc
        out = [
            remote(total.at[it], rhs.at[it, s], send3.at[it, d], rec3.at[it, d], sub_peer(d))
            for d in range(1, n_sub)
        ]
        pending.extend(out)
        return out

    def finish_coarse(it, copies):
        for copy in copies:
            copy.wait_recv()
        whole = jnp.concatenate(
            [
                jnp.concatenate([rhs[it, 8 * h + lg] for lg in range(8)], axis=0)
                for h in range(2)
            ],
            axis=1,
        )
        both = stacked(whole)
        pair = dot_nt(both, jnp.concatenate([near_inverse[0], near_inverse[1]], axis=0))
        picked = pair[:load_cases, :128] + pair[:load_cases, 128:] + pair[load_cases:, :128]
        low = dot_nt(both, inv_hi[...])
        low = low[:load_cases] + low[load_cases:] + dot_nt(both[:load_cases], inv_lo[...])
        return picked, low

    def spread_coarse(picked, f):
        both = stacked(picked)
        out = dot(both, wide_g[0, :, faces(f)])
        return out[:load_cases] + out[load_cases:] + dot(both[:load_cases], wide_g[1, :, faces(f)])

    def row_of(a, b):
        return jnp.sum(jnp.concatenate([a, b], axis=0).T, axis=0, keepdims=True)

    def start_small(it, rows):
        for i, r in enumerate(rows):
            small[it, i : i + 1, :] = r
        copies = [
            remote(small.at[it], small_recv1.at[it, d], ssend1.at[it, d], srec1.at[it, d], grp_peer(d))
            for d in range(1, n_grp)
        ]
        pending.extend(copies)
        return copies

    def middle_small(it, copies):
        acc = small[it]
        for d in range(1, n_grp):
            copies[d - 1].wait_recv()
            acc = acc + small_recv1[it, d]
        small2[it] = acc
        out = [
            remote(small2.at[it], small_recv2.at[it, d], ssend2.at[it, d], srec2.at[it, d], sub_peer(d))
            for d in range(1, n_sub)
        ]
        pending.extend(out)
        return out

    def finish_small(it, copies, count):
        acc = small2[it]
        for d in range(1, n_sub):
            copies[d - 1].wait_recv()
            acc = acc + small_recv2[it, d]
        out = []
        for i in range(count):
            turned = jnp.broadcast_to(acc[i : i + 1, :], (128, 128)).T
            out += [turned[:load_cases], turned[load_cases:]]
        return out

    def tile(a):
        return jnp.concatenate([a] * (face // 128), axis=1)

    small[...] = jnp.zeros(small.shape, F32)
    y0 = y_buf[0]
    coarse = start_coarse(0, y0)
    rz_lanes = lane_chunks(0.5 * res[...] * y0)

    for f in range(4):
        z0[:, faces(f)] = 0.5 * (y_buf[0, :, faces(f)] - neighbour(1, f))
    direction = z0[...].astype(BF16)
    flex_copy.wait()
    for h in range(2):
        cut = slice(half * h, half * h + half)
        free0[:, cut] = dot(direction, flex[:, cut])
        send_out(2, 2 * h, free0)
    little = start_small(0, [row_of(rz_lanes, lane_chunks(z0[...] * free0[...]))])
    coarse = middle_coarse(0, coarse)

    inverse_copy.wait()
    hi, lo = split(inverse[...])
    inv_hi[...] = hi
    inv_lo[...] = lo
    chosen_hi = dot_nt(select[...], inv_hi[...]).astype(BF16)
    chosen_lo = dot_nt(select[...], inv_lo[...]).astype(BF16)
    columns = (
        dot(chosen_hi, inv_hi[...]) + dot(chosen_lo, inv_hi[...]) + dot(chosen_hi, inv_lo[...])
    )
    hi, lo = split(columns)
    near_inverse[0] = hi
    near_inverse[1] = lo

    little = middle_small(0, little)
    for f in range(4):
        image0[:, faces(f)] = free0[:, faces(f)] - neighbour(2, f)
    coarse = last_coarse(0, coarse)
    rz0, free_curv = finish_small(0, little, 1)
    picked, low0 = finish_coarse(0, coarse)
    curv0 = free_curv + jnp.sum(low0 * low0, axis=1, keepdims=True)
    a0 = rz0 / curv0
    for f in range(4):
        image0[:, faces(f)] = image0[:, faces(f)] + spread_coarse(picked, f)
        res[:, faces(f)] = res[:, faces(f)] - tile(a0) * image0[:, faces(f)]

    apply_schur(3)
    y1 = y_buf[1]
    coarse = start_coarse(1, y1)
    rz_lanes = lane_chunks(0.5 * res[...] * y1)
    for f in range(4):
        mult_out[:, faces(f)] = 0.5 * (y_buf[1, :, faces(f)] - neighbour(3, f))
    direction = mult_out[...].astype(BF16)
    for h in range(2):
        cut = slice(half * h, half * h + half)
        free1[:, cut] = dot(direction, flex[:, cut])
        send_out(4, 2 * h, free1)
    z1 = mult_out[...]
    little = start_small(
        1,
        [
            row_of(rz_lanes, lane_chunks(z1 * free1[...])),
            row_of(lane_chunks(z1 * free0[...]), jnp.zeros((load_cases, 128), F32)),
        ],
    )
    coarse = middle_coarse(1, coarse)
    little = middle_small(1, little)
    for f in range(4):
        res_out[:, faces(f)] = free1[:, faces(f)] - neighbour(4, f)
    coarse = last_coarse(1, coarse)
    rz1, curv_11, curv_10, _ = finish_small(1, little, 2)
    picked, low1 = finish_coarse(1, coarse)
    beta = rz1 / rz0
    low = low1 + beta[:, 0:1] * low0
    curv1 = curv_11 + 2.0 * beta * curv_10 + beta * beta * free_curv + jnp.sum(low * low, axis=1, keepdims=True)
    a1 = rz1 / curv1
    for f in range(4):
        sign = 1.0 if f % 2 else -1.0
        image = res_out[:, faces(f)] + spread_coarse(picked, f) + tile(beta) * image0[:, faces(f)]
        res_out[:, faces(f)] = sign * (res[:, faces(f)] - tile(a1) * image)
        mult_out[:, faces(f)] = sign * (
            tile(a1) * mult_out[:, faces(f)] + tile(a0 + a1 * beta) * z0[:, faces(f)]
        )
    for copy in pending:
        copy.wait_send()


def solution(mesh):
    n_sub, n_grp = mesh.shape["sub"], mesh.shape["grp"]

    def shards(loads, flex, schur, coupling, inverse, match, corner):
        load_cases, interface = loads.shape[2:]
        face = interface // 4
        corners, size = coupling.shape[2], inverse.shape[0]
        vmem, dma = pltpu.VMEM, pltpu.SemaphoreType.DMA
        flat = (load_cases, interface)
        block = (8, size // 2)
        scratch = [
            vmem(flat, F32), vmem((interface, interface), BF16), vmem((interface, interface), BF16),
            vmem((corners, interface), F32), vmem((size, size), F32), vmem((4, face), jnp.int32),
            vmem(corner.shape, jnp.int32), vmem((8, 128), jnp.int32),
            vmem((5, 4, load_cases, face), F32), vmem((4, corners, face), F32), vmem((4, 8, 128), jnp.int32),
            vmem((4, face, face), BF16), vmem((2, 128, interface), BF16), vmem((128, size), BF16),
            vmem((2, 128, size), BF16), vmem((size, size), BF16), vmem((size, size), BF16),
            vmem((2,) + flat, F32), vmem(flat, F32), vmem(flat, F32), vmem(flat, F32), vmem(flat, F32),
            vmem(flat, F32),
            vmem((2, n_sub) + block, F32), vmem((2, n_sub) + block, F32), vmem((2,) + block, F32),
            vmem((2, n_grp) + block, F32), vmem((2,) + block, F32), vmem((2, n_sub) + block, F32),
            vmem((2, 8, 128), F32), vmem((2, n_grp, 8, 128), F32), vmem((2, 8, 128), F32),
            vmem((2, n_sub, 8, 128), F32),
            dma((7,)), dma((5, 4)), dma((5, 4)), dma((2, 4)), dma((2, 4)),
            dma((2, n_sub)), dma((2, n_sub)), dma((2, n_grp)), dma((2, n_grp)), dma((2, n_sub)), dma((2, n_sub)),
            dma((2, n_grp)), dma((2, n_grp)), dma((2, n_sub)), dma((2, n_sub)),
        ]
        out = pl.pallas_call(
            functools.partial(kernel, n_sub, n_grp),
            out_shape=(jax.ShapeDtypeStruct(flat, F32), jax.ShapeDtypeStruct(flat, F32)),
            in_specs=[ANY] * 7,
            out_specs=(VMEM, VMEM),
            scratch_shapes=scratch,
            compiler_params=pltpu.CompilerParams(
                collective_id=0, has_side_effects=True, vmem_limit_bytes=48 * 2**20
            ),
            name="cg",
        )(loads, flex, schur, coupling, inverse, match, corner)
        return tuple(x.reshape(1, 1, load_cases, 4, face) for x in out)

    split4 = P("sub", "grp", None, None)
    return jax.shard_map(
        shards,
        mesh=mesh,
        in_specs=(split4, split4, split4, split4, P(), split4, P("sub", "grp", None)),
        out_specs=(P("sub", "grp", None, None, None), P("sub", "grp", None, None, None)),
        check_vma=False,
    )
```

time: 915 us -> 74.3 us (0.08)
  waiting for transfers between devices: 486 us -> 0 us
  blocking collectives: 226 us -> 0 us
  local copies, waits for them, and re-layouts: 96.5 us -> 6.64 us
  Pallas kernels: 0 us -> 66.8 us
  matrix products: 31.8 us -> 0 us
  starting transfers between devices: 30 us -> 0 us
  other arithmetic: 27.9 us -> 0 us
  between operations: 14.7 us -> 0.65 us
    psum x2 -> x0, waiting for transfers between devices: 486 us -> none  [shards(): apply_coarse_total = lax.psum(share, ('sub', 'grp'))]
    psum x3 -> x0, blocking collectives: 226 us -> none  [the longest x2 151 us: inner(): return lax.psum(0.5 * jnp.sum(former * latter, axis=(1, 2)), ('sub', 'grp'))]
    pallas_call x0 -> x1, Pallas kernels: none -> 66.8 us  [shards(): pl.pallas_call(functools.partial(kernel, n_sub, n_grp), out_shape=(jax.Sh...]
    gather x40 -> x0, local copies, waits for them, and re-layouts: 47 us -> none  [the longest x10 12.4 us: neighbour_jump(): from_left_grp = jnp.take(around_grp[:, 0], matching[2], axis=1)]
    dot_general x16 -> x0, matrix products: 31.8 us -> none  [the longest x2 8.63 us: shards(): jnp.dot(forces.astype(jnp.bfloat16), flex_local, preferred_element_type=j...]
    ppermute x20 -> x0, starting transfers between devices: 29.7 us -> none  [the longest x10 15.8 us: extended(): after = lax.ppermute(first, axis, down)]
    squeeze x20 -> x0, local copies, waits for them, and re-layouts: 19.5 us -> none  [the longest x5 5.1 us: neighbour_jump(): from_left_grp = jnp.take(around_grp[:, 0], matching[2], axis=1)]
    another operation x14 -> x0, other arithmetic: 13.7 us -> none  [neighbour_jump(): jnp.stack([from_left_sub - displaced[:, 0], displaced[:, 1] - from_right_...]
  transfers between devices with their start and end apart: 22 -> 0, of which waited for: 3 -> 0; matrix products, arithmetic and copies ran while one was open for 8% -> 0% of each run, Pallas kernels for 0% -> 0%
where the time goes in v1:
time: 74.3 us; the launch traced here: 74.1 us
  Pallas kernels  66.8 us (90%)
  local copies, waits for them, and re-layouts  6.64 us (9%)
    pallas_call x1, Pallas kernels, shards(): pl.pallas_call(functools.partial(kernel, n_sub, n_grp), out_shape=(jax.Sh...  66.8 us
    unnamed x9, local copies, waits for them, and re-layouts  4.9 us
    reshape x2, local copies, waits for them, and re-layouts, shards(): return tuple((x.reshape(1, 1, load_cases, 4, face) for x in out))  1.75 us

profile of v1, /device:TPU:1, one launch (start us, length us, event | category | flops | bytes accessed | tf_op | source)
XLA Modules:
  0.0 74.1 jit_solution(12131759504047298054)
XLA Ops:
  0.6 0.9 %copy.9.coupling_hbm = f32[1,1,12,1536]{3,2,1,0:T(8,128)S(1)} copy(f32[1,1,12,1536]{3,1,2,0:T(1,128)} %param.10) | data formatting | bytes 147456 | tf_op args[3]
  1.5 0.0 copy-start
  1.5 1.7 %copy-done = f32[768,768]{1,0:T(8,128)S(1)} copy-done((f32[768,768]{1,0:T(8,128)S(1)}, f32[768,768]{1,0:T(8,128)}, u32[]{:S(2)}) %copy-start) | copy-done | bytes 2359320
  3.2 0.0 copy-start.1
  3.2 1.0 %copy-done.1 = f32[1,1,64,1536]{3,2,1,0:T(8,128)S(1)} copy-done((f32[1,1,64,1536]{3,2,1,0:T(8,128)S(1)}, f32[1,1,64,1536]{3,2,1,0:T(8,128)}, u32[]{:S(2)}) %copy-start.1) | copy-done | bytes 393240
  4.2 0.0 copy-start.2
  4.2 0.7 copy-done.2
  4.9 0.0 copy-start.3
  4.9 0.7 copy-done.3
  5.5 66.8 %cg.1 = (f32[64,1536]{1,0:T(8,128)S(1)}, f32[64,1536]{1,0:T(8,128)S(1)}) custom-call(f32[1,1,64,1536]{3,2,1,0:T(8,128)S(1)} %copy-done.1, bf16[1,1,1536,1536]{3,2,1,0:T(8,128)(2,1)} %flex_hbm.1, bf16[1,1,1536,1536]{3,2,1,0:T(8,128)(2,1)} %schur_hbm.1, f32[1,1,12,1536]{3,2,1,0:T(8,128)S(1)} %copy.9.coupling_hbm, f32[768,768]{1,0:T(8,128)S(1)} %copy-done, ...), custom_call_target="tpu_custom_call" | custom-call | tf_op jit(solution)/shard_map/cg/pallas_call | solution.py:389
  72.3 0.9 %reshape.10 = f32[1,1,64,4,384]{4,3,2,1,0:T(4,128)} reshape(f32[64,1536]{1,0:T(8,128)S(1)} %get-tuple-element.4) | data formatting | bytes 786432 | tf_op jit(solution)/shard_map/reshape | solution.py:400
  73.2 0.9 %reshape.11 = f32[1,1,64,4,384]{4,3,2,1,0:T(4,128)} reshape(f32[64,1536]{1,0:T(8,128)S(1)} %get-tuple-element.5) | data formatting | bytes 786432 | tf_op jit(solution)/shard_map/reshape | solution.py:400
Async XLA Ops:
  1.5 1.7 %copy-start = (f32[768,768]{1,0:T(8,128)S(1)}, f32[768,768]{1,0:T(8,128)}, u32[]{:S(2)}) copy-start(f32[768,768]{1,0:T(8,128)} %inverse_hbm.1) | copy-start | bytes 7077892
  3.2 1.0 %copy-start.1 = (f32[1,1,64,1536]{3,2,1,0:T(8,128)S(1)}, f32[1,1,64,1536]{3,2,1,0:T(8,128)}, u32[]{:S(2)}) copy-start(f32[1,1,64,1536]{3,2,1,0:T(8,128)} %loads_hbm.1) | copy-start | bytes 1179652
  4.2 0.7 copy-start.2
  4.9 0.7 copy-start.3

commit v2 on v0

v2 whole, which is shorter than its diff:
```python
import functools

import jax
import jax.numpy as jnp
from jax import lax
from jax.experimental import pallas as pl
from jax.experimental.pallas import tpu as pltpu
from jax.sharding import PartitionSpec as P

MESH = pl.DeviceIdType.MESH
F32 = jnp.float32
BF16 = jnp.bfloat16
OPPOSITE = (1, 0, 3, 2)
HBM = pl.BlockSpec(memory_space=pltpu.HBM)
VMEM = pl.BlockSpec(memory_space=pltpu.VMEM)
NT = (((1,), (1,)), ((), ()))
SIDE = 4
FAR_FIRST = sorted(range(1, 16), key=lambda k: -(2 - abs(2 - k // 4)) - (2 - abs(2 - k % 4)))
RING = (4, 3, 5, 2, 6, 1, 7)


def dot(a, b):
    return jnp.dot(a, b, preferred_element_type=F32)


def dot_nt(a, b):
    return lax.dot_general(a, b, NT, preferred_element_type=F32)


def split(x):
    high = x.astype(BF16)
    return high, (x - high.astype(F32)).astype(BF16)


def stacked(x):
    return jnp.concatenate(split(x), axis=0)


def lane_chunks(x):
    total = x[:, 0:128]
    for c in range(1, x.shape[1] // 128):
        total = total + x[:, 128 * c : 128 * c + 128]
    return total


def kernel(
    n_sub, n_grp,
    loads_hbm, flex_hbm, schur_hbm, coupling_hbm, inverse_hbm, match_hbm, corner_hbm,
    mult_out, res_out,
    loads, flex, schur, coupling, inverse, match, corner, corner_pad,
    halo, near_coupling, near_corner,
    perm, padded, wide_g, schur_g, select, near_inverse, inv_hi, inv_lo,
    res, y_buf, free, z_buf, image,
    dense, recv1, part, chip, pair, recv2, total, rhs,
    local_sem, halo_send, halo_recv, near_send, near_recv,
    send1, rec1, send2, rec2, send3, rec3,
):
    s, g = lax.axis_index("sub"), lax.axis_index("grp")
    load_cases, interface = loads.shape
    face = interface // 4
    half = interface // 2
    size = inverse.shape[0]
    width = size // 2
    plain, wide = slice(0, width), slice(0, width + 128)
    corners = coupling.shape[0]
    row, column = s // SIDE, lax.rem(s, SIDE)
    rows_on = [lax.rem(row + d, SIDE) * SIDE for d in range(SIDE)]
    columns_on = [lax.rem(column + d, SIDE) for d in range(SIDE)]

    def sub_peer(k):
        return (rows_on[k // SIDE] + columns_on[k % SIDE], g)

    def z_peer(d):
        return (s, lax.rem(g + 2 * d, n_grp))

    other = (s, g + 1 - 2 * lax.rem(g, 2))
    near = (
        (lax.rem(s + n_sub - 1, n_sub), g), (lax.rem(s + 1, n_sub), g),
        (s, lax.rem(g + n_grp - 1, n_grp)), (s, lax.rem(g + 1, n_grp)),
    )

    def faces(f):
        return slice(face * f, face * f + face)

    def remote(src, dst, send, recv, to):
        pltpu.make_async_remote_copy(
            src_ref=src, dst_ref=dst, send_sem=send, recv_sem=recv, device_id=to, device_id_type=MESH
        ).start()

    def drain(ref, sem):
        pltpu.make_async_copy(ref, ref, sem).wait()

    sent = []

    def flush():
        for ref, sem in sent:
            drain(ref, sem)
        sent.clear()

    barrier = pltpu.get_barrier_semaphore()
    for d in range(1, n_sub):
        to = (lax.rem(s + d, n_sub), g)
        pl.semaphore_signal(barrier, inc=1, device_id=to, device_id_type=MESH)
    for d in RING:
        pl.semaphore_signal(barrier, inc=1, device_id=z_peer(d), device_id_type=MESH)
    for d in (1, n_grp - 1):
        to = (s, lax.rem(g + d, n_grp))
        pl.semaphore_signal(barrier, inc=1, device_id=to, device_id_type=MESH)

    sources = (
        (corner_hbm, corner), (coupling_hbm.at[0], coupling), (loads_hbm.at[0, 0], loads),
        (match_hbm.at[0, 0], match), (schur_hbm.at[0, 0], schur), (flex_hbm.at[0, 0], flex), (inverse_hbm, inverse),
    )
    local = []
    for i, (src, dst) in enumerate(sources):
        copy = pltpu.make_async_copy(src, dst, local_sem.at[i])
        copy.start()
        local.append(copy)
    corner_copy, coupling_copy, loads_copy, match_copy, schur_copy, flex_copy, inverse_copy = local

    corner_copy.wait()
    corner_pad[...] = jnp.full(corner_pad.shape, -1, jnp.int32)
    corner_pad[0:1, 0:corners] = corner[0]
    coupling_copy.wait()
    loads_copy.wait()
    pl.semaphore_wait(barrier, n_sub - 1 + len(RING) + 2)

    for f in range(4):
        o = OPPOSITE[f]
        remote(coupling.at[:, :, faces(f)], near_coupling.at[o], near_send.at[0], near_recv.at[0], near[f])
    sent.append((near_coupling, near_send.at[0]))

    def send_out(step, f0, ref):
        for f in (f0, f0 + 1):
            o = OPPOSITE[f]
            remote(ref.at[:, faces(f)], halo.at[step, o], halo_send.at[step, f0 // 2], halo_recv.at[step, f0 // 2], near[f])
        sent.append((halo.at[step, f0 : f0 + 2], halo_send.at[step, f0 // 2]))

    send_out(0, 0, loads)
    send_out(0, 2, loads)
    for f in range(4):
        remote(corner_pad, near_corner.at[OPPOSITE[f]], near_send.at[1], near_recv.at[1], near[f])
    sent.append((near_corner, near_send.at[1]))

    match_copy.wait()
    index = lax.broadcasted_iota(jnp.int32, (face, face), 0)
    for f in range(4):
        perm[f] = (index == match[f : f + 1, :]).astype(BF16)

    def neighbour(step, f):
        if f % 2 == 0:
            drain(halo.at[step, f : f + 2], halo_recv.at[step, f // 2])
        both = dot(stacked(halo[step, f]), perm[f])
        return both[:load_cases] + both[load_cases:]

    wide_g[...] = jnp.zeros(wide_g.shape, BF16)
    padded[...] = jnp.zeros(padded.shape, F32)
    for k in range(corners):
        padded[k : k + 1, :] = coupling[k]
    hi, lo = split(padded[...])
    wide_g[0:16, :] = hi
    wide_g[128:144, :] = lo
    drain(near_coupling, near_recv.at[0])
    for f in range(4):
        for k in range(corners):
            padded[k : k + 1, faces(f)] = near_coupling[f, k]
        both = -dot(stacked(padded[:, faces(f)]), perm[f])
        start = 16 * f + 16
        wide_g[start : start + 16, faces(f)] = both[:16].astype(BF16)
        wide_g[start + 128 : start + 144, faces(f)] = both[16:].astype(BF16)
    schur_copy.wait()
    for f in range(4):
        both = dot_nt(schur[faces(f), :], wide_g[...])
        hi, lo = split(0.5 * (both[:, :128] + both[:, 128:]))
        schur_g[faces(f), 0:128] = hi
        schur_g[faces(f), 128:256] = lo

    drain(near_corner, near_recv.at[1])
    lane = lax.broadcasted_iota(jnp.int32, (8, 128), 1)
    numbers = jnp.where(lane < corners, corner_pad[...], -1)
    for f in range(4):
        start = 16 * f + 16
        inside = jnp.logical_and(lane >= start, lane < start + corners)
        numbers = jnp.where(inside, pltpu.roll(near_corner[f], start, 1), numbers)
    turned = jnp.broadcast_to(numbers.astype(F32)[0:1, :], (128, 128)).T
    unknown = lax.broadcasted_iota(jnp.int32, (128, size), 1).astype(F32)
    select[...] = (turned[:, 0:1] == unknown).astype(BF16)

    def start_coarse(it, both):
        spread = dot(stacked(both[:, :128] + both[:, 128:]), select[...])
        spread = spread[:load_cases] + spread[load_cases:]
        for t in range(n_sub):
            lg, h = t % 8, t // 8
            dense[it, t] = spread[8 * lg : 8 * lg + 8, width * h : width * h + width]
        for k in FAR_FIRST:
            to = sub_peer(k)
            remote(dense.at[it, to[0]], recv1.at[it, k - 1], send1.at[it], rec1.at[it], to)
        sent.append((recv1.at[it], send1.at[it]))

    def middle_coarse(it, cut):
        drain(recv1.at[it], rec1.at[it])
        acc = dense[it, s]
        for k in range(1, n_sub):
            acc = acc + recv1[it, k - 1]
        part[it, :, :width] = acc
        remote(part.at[it, :, cut], chip.at[it, :, cut], send2.at[it, 0], rec2.at[it, 0], other)
        sent.append((chip.at[it, :, cut], send2.at[it, 0]))

    def third_coarse(it, cut):
        drain(chip.at[it, :, cut], rec2.at[it, 0])
        pair[it, :, cut] = part[it, :, cut] + chip[it, :, cut]
        for d in RING:
            remote(pair.at[it, :, cut], recv2.at[it, d - 1, :, cut], send2.at[it, 1], rec2.at[it, 1], z_peer(d))
        sent.append((recv2.at[it, :, :, cut], send2.at[it, 1]))

    def last_coarse(it, cut):
        drain(recv2.at[it, :, :, cut], rec2.at[it, 1])
        acc = pair[it, :, cut]
        for d in RING:
            acc = acc + recv2[it, d - 1, :, cut]
        total[it, :, cut] = acc
        rhs[it, s, :, cut] = acc
        for k in FAR_FIRST:
            remote(total.at[it, :, cut], rhs.at[it, s, :, cut], send3.at[it], rec3.at[it], sub_peer(k))
        sent.append((rhs.at[it, 0 : n_sub - 1, :, cut], send3.at[it]))

    def whole_coarse(it, cut):
        drain(rhs.at[it, 0 : n_sub - 1, :, cut], rec3.at[it])
        return stacked(
            jnp.concatenate(
                [
                    jnp.concatenate([rhs[it, 8 * h + lg, :, :width] for lg in range(8)], axis=0)
                    for h in range(2)
                ],
                axis=1,
            )
        )

    def pick(both):
        out = dot_nt(both, near_inverse[...])
        return out[:load_cases, :128] + out[:load_cases, 128:] + out[load_cases:, :128]

    def lowered(both):
        low = dot_nt(both, inv_hi[...])
        return low[:load_cases] + low[load_cases:] + dot_nt(both[:load_cases], inv_lo[...])

    def spread_coarse(both, f):
        out = dot(both, wide_g[0:128, faces(f)])
        return out[:load_cases] + out[load_cases:] + dot(both[:load_cases], wide_g[128:256, faces(f)])

    def row_of(a, b):
        return jnp.sum(jnp.concatenate([a, b], axis=0).T, axis=0, keepdims=True)

    def tile(a):
        return jnp.concatenate([a] * (face // 128), axis=1)

    def apply_schur(it, weighted):
        for h in range(2):
            cut = slice(half * h, half * h + half)
            y_buf[it, :, cut] = dot(weighted, schur[:, cut])
            send_out(2 * it + 1, 2 * h, y_buf.at[it])

    def start_flex(it):
        for f in (2, 3):
            z_buf[it, :, faces(f)] = 0.5 * (y_buf[it, :, faces(f)] - neighbour(2 * it + 1, f))
        free[it] = dot(z_buf[it, :, half:].astype(BF16), flex[half:, :])

    def finish_flex(it):
        for f in (0, 1):
            z_buf[it, :, faces(f)] = 0.5 * (y_buf[it, :, faces(f)] - neighbour(2 * it + 1, f))
        direction = z_buf[it, :, :half].astype(BF16)
        for h in range(2):
            cut = slice(half * h, half * h + half)
            free[it, :, cut] = free[it, :, cut] + dot(direction, flex[:half, cut])
            send_out(2 * it + 2, 2 * h, free.at[it])

    for f in (2, 3):
        res[:, faces(f)] = loads[:, faces(f)] - neighbour(0, f)
    both = dot((0.5 * res[:, half:]).astype(BF16), schur_g[half:, :])
    for f in (0, 1):
        res[:, faces(f)] = loads[:, faces(f)] - neighbour(0, f)
    weighted = (0.5 * res[...]).astype(BF16)
    start_coarse(0, both + dot(weighted[:, :half], schur_g[:half, :]))
    apply_schur(0, weighted)

    inverse_copy.wait()
    hi, lo = split(inverse[...])
    inv_hi[...] = hi
    inv_lo[...] = lo
    chosen_hi = dot_nt(select[...], inv_hi[...]).astype(BF16)
    chosen_lo = dot_nt(select[...], inv_lo[...]).astype(BF16)
    hi, lo = split(dot(chosen_hi, inv_hi[...]) + dot(chosen_lo, inv_hi[...]) + dot(chosen_hi, inv_lo[...]))
    near_inverse[0:128, :] = hi
    near_inverse[128:256, :] = lo
    flex_copy.wait()

    middle_coarse(0, plain)
    start_flex(0)
    third_coarse(0, plain)
    finish_flex(0)
    rows = [row_of(lane_chunks(0.5 * res[...] * y_buf[0]), lane_chunks(z_buf[0] * free[0]))]
    flush()
    last_coarse(0, plain)
    for f in range(4):
        image[0, :, faces(f)] = free[0, :, faces(f)] - neighbour(2, f)
    both_rhs = whole_coarse(0, plain)
    both = stacked(pick(both_rhs))
    for f in range(4):
        image[0, :, faces(f)] = image[0, :, faces(f)] + spread_coarse(both, f)

    weighted = (0.5 * image[0]).astype(BF16)
    apply_schur(1, weighted)
    start_coarse(1, dot(weighted, schur_g[...]))
    low0 = lowered(both_rhs)
    rows.append(
        row_of(
            lane_chunks(0.5 * (image[0] * y_buf[0] + res[...] * y_buf[1])),
            lane_chunks(0.5 * image[0] * y_buf[1]),
        )
    )
    part[1, :, width:] = jnp.zeros((8, 128), F32)
    flush()
    start_flex(1)
    finish_flex(1)
    rows.append(
        row_of(
            lane_chunks(z_buf[1] * free[0] + z_buf[0] * free[1]),
            lane_chunks(z_buf[1] * free[1]),
        )
    )
    for i, r in enumerate(rows):
        part[1, i : i + 1, width:] = r
    middle_coarse(1, wide)
    third_coarse(1, wide)
    for f in range(4):
        image[1, :, faces(f)] = free[1, :, faces(f)] - neighbour(4, f)
    flush()
    last_coarse(1, wide)
    flush()
    both_rhs = whole_coarse(1, wide)
    both = stacked(pick(both_rhs))
    low1 = lowered(both_rhs)

    acc = rhs[1, 0, :, width:]
    for k in range(1, n_sub):
        acc = acc + rhs[1, k, :, width:]
    sums = []
    for i in range(len(rows)):
        turned = jnp.broadcast_to(acc[i : i + 1, :], (128, 128)).T
        sums += [turned[:load_cases], turned[load_cases:]]
    rz0, free_00, res_01, res_11, free_01, free_11 = sums
    a0 = rz0 / (free_00 + jnp.sum(low0 * low0, axis=1, keepdims=True))
    rz1 = rz0 - a0 * res_01 + a0 * a0 * res_11
    more = 1.0 + rz1 / rz0
    low = more[:, 0:1] * low0 - a0[:, 0:1] * low1
    curvature = (
        more * more * free_00 - more * a0 * free_01 + a0 * a0 * free_11 + jnp.sum(low * low, axis=1, keepdims=True)
    )
    a1 = rz1 / curvature
    first, second = a0 + a1 * more, a0 * a1
    for f in range(4):
        sign = 1.0 if f % 2 else -1.0
        one, two = tile(sign * first), tile(sign * second)
        mult_out[:, faces(f)] = one * z_buf[0, :, faces(f)] - two * z_buf[1, :, faces(f)]
        res_out[:, faces(f)] = (
            sign * res[:, faces(f)]
            - one * image[0, :, faces(f)]
            + two * (image[1, :, faces(f)] + spread_coarse(both, f))
        )


def solution(mesh):
    n_sub, n_grp = mesh.shape["sub"], mesh.shape["grp"]

    def shards(loads, flex, schur, coupling, inverse, match, corner):
        load_cases, interface = loads.shape[2:]
        face = interface // 4
        corners, size = coupling.shape[2], inverse.shape[0]
        vmem, dma = pltpu.VMEM, pltpu.SemaphoreType.DMA
        flat = (load_cases, interface)
        block, wide = (8, size // 2), (8, size // 2 + 128)
        scratch = [
            vmem(flat, F32), vmem((interface, interface), BF16), vmem((interface, interface), BF16),
            vmem((corners, 1, interface), F32), vmem((size, size), F32), vmem((4, face), jnp.int32),
            vmem(corner.shape, jnp.int32), vmem((8, 128), jnp.int32),
            vmem((5, 4, load_cases, face), F32), vmem((4, corners, 1, face), F32), vmem((4, 8, 128), jnp.int32),
            vmem((4, face, face), BF16), vmem((16, interface), F32), vmem((256, interface), BF16),
            vmem((interface, 256), BF16), vmem((128, size), BF16),
            vmem((256, size), BF16), vmem((size, size), BF16), vmem((size, size), BF16),
            vmem(flat, F32), vmem((2,) + flat, F32), vmem((2,) + flat, F32), vmem((2,) + flat, F32),
            vmem((2,) + flat, F32),
            vmem((2, n_sub) + block, F32), vmem((2, n_sub - 1) + block, F32), vmem((2,) + wide, F32),
            vmem((2,) + wide, F32), vmem((2,) + wide, F32), vmem((2, len(RING)) + wide, F32), vmem((2,) + wide, F32),
            vmem((2, n_sub) + wide, F32),
            dma((7,)), dma((5, 2)), dma((5, 2)), dma((2,)), dma((2,)),
            dma((2,)), dma((2,)), dma((2, 2)), dma((2, 2)), dma((2,)), dma((2,)),
        ]
        out = pl.pallas_call(
            functools.partial(kernel, n_sub, n_grp),
            out_shape=(jax.ShapeDtypeStruct(flat, F32), jax.ShapeDtypeStruct(flat, F32)),
            in_specs=[HBM] * 7,
            out_specs=(VMEM, VMEM),
            scratch_shapes=scratch,
            compiler_params=pltpu.CompilerParams(
                collective_id=0, has_side_effects=True, vmem_limit_bytes=48 * 2**20
            ),
            name="cg",
        )(
            *(
                pltpu.with_memory_space_constraint(x, pltpu.HBM)
                for x in (loads, flex, schur, coupling.transpose(0, 2, 1, 3), inverse, match, corner)
            )
        )
        return tuple(x.reshape(1, 1, load_cases, 4, face) for x in out)

    split4 = P("sub", "grp", None, None)
    return jax.shard_map(
        shards,
        mesh=mesh,
        in_specs=(split4, split4, split4, split4, P(), split4, P("sub", "grp", None)),
        out_specs=(P("sub", "grp", None, None, None), P("sub", "grp", None, None, None)),
        check_vma=False,
    )
```

time: 915 us -> 58.4 us (0.06)
  waiting for transfers between devices: 486 us -> 0 us
  blocking collectives: 226 us -> 0 us
  local copies, waits for them, and re-layouts: 96.5 us -> 1.75 us
  Pallas kernels: 0 us -> 56 us
  matrix products: 31.8 us -> 0 us
  starting transfers between devices: 30 us -> 0 us
  other arithmetic: 27.9 us -> 0 us
  between operations: 14.7 us -> 0.64 us
    psum x2 -> x0, waiting for transfers between devices: 486 us -> none  [shards(): apply_coarse_total = lax.psum(share, ('sub', 'grp'))]
    psum x3 -> x0, blocking collectives: 226 us -> none  [the longest x2 151 us: inner(): return lax.psum(0.5 * jnp.sum(former * latter, axis=(1, 2)), ('sub', 'grp'))]
    pallas_call x0 -> x1, Pallas kernels: none -> 56 us  [shards(): pl.pallas_call(functools.partial(kernel, n_sub, n_grp), out_shape=(jax.Sh...]
    gather x40 -> x0, local copies, waits for them, and re-layouts: 47 us -> none  [the longest x10 12.4 us: neighbour_jump(): from_left_grp = jnp.take(around_grp[:, 0], matching[2], axis=1)]
    dot_general x16 -> x0, matrix products: 31.8 us -> none  [the longest x2 8.63 us: shards(): jnp.dot(forces.astype(jnp.bfloat16), flex_local, preferred_element_type=j...]
    ppermute x20 -> x0, starting transfers between devices: 29.7 us -> none  [the longest x10 15.8 us: extended(): after = lax.ppermute(first, axis, down)]
    squeeze x20 -> x0, local copies, waits for them, and re-layouts: 19.5 us -> none  [the longest x5 5.1 us: neighbour_jump(): from_left_grp = jnp.take(around_grp[:, 0], matching[2], axis=1)]
    another operation x14 -> x0, other arithmetic: 13.7 us -> none  [neighbour_jump(): jnp.stack([from_left_sub - displaced[:, 0], displaced[:, 1] - from_right_...]
  transfers between devices with their start and end apart: 22 -> 0, of which waited for: 3 -> 0; matrix products, arithmetic and copies ran while one was open for 8% -> 0% of each run, Pallas kernels for 0% -> 0%
where the time goes in v2:
time: 58.4 us
  Pallas kernels  56 us (96%)
  local copies, waits for them, and re-layouts  1.75 us (3%)
  between operations  0.64 us (1%)
    pallas_call x1, Pallas kernels, shards(): pl.pallas_call(functools.partial(kernel, n_sub, n_grp), out_shape=(jax.Sh...  56 us
    reshape x2, local copies, waits for them, and re-layouts, shards(): return tuple((x.reshape(1, 1, load_cases, 4, face) for x in out))  1.75 us

profile of v2, /device:TPU:1, one launch (start us, length us, event | category | flops | bytes accessed | tf_op | source)
XLA Modules:
  0.0 58.4 jit_solution(16104682881397171947)
XLA Ops:
  0.6 56.0 %cg.1 = (f32[64,1536]{1,0:T(8,128)S(1)}, f32[64,1536]{1,0:T(8,128)S(1)}) custom-call(f32[1,1,64,1536]{3,2,1,0:T(8,128)} %loads_hbm.1, bf16[1,1,1536,1536]{3,2,1,0:T(8,128)(2,1)} %flex_hbm.1, bf16[1,1,1536,1536]{3,2,1,0:T(8,128)(2,1)} %schur_hbm.1, f32[1,12,1,1536]{3,2,1,0:T(1,128)} %bitcast.1, f32[768,768]{1,0:T(8,128)} %inverse_hbm.1, ...), custom_call_target="tpu_custom_call" | custom-call | tf_op jit(solution)/shard_map/cg/pallas_call | solution.py:398
  56.6 0.9 %reshape.10 = f32[1,1,64,4,384]{4,3,2,1,0:T(4,128)} reshape(f32[64,1536]{1,0:T(8,128)S(1)} %get-tuple-element.4) | data formatting | bytes 786432 | tf_op jit(solution)/shard_map/reshape | solution.py:414
  57.5 0.9 %reshape.11 = f32[1,1,64,4,384]{4,3,2,1,0:T(4,128)} reshape(f32[64,1536]{1,0:T(8,128)S(1)} %get-tuple-element.5) | data formatting | bytes 786432 | tf_op jit(solution)/shard_map/reshape | solution.py:414

commit v3 on v2

--- a/solution.py
+++ b/solution.py
@@ -46,10 +46,10 @@
 def kernel(
     n_sub, n_grp,
     loads_hbm, flex_hbm, schur_hbm, coupling_hbm, inverse_hbm, match_hbm, corner_hbm,
-    mult_out, res_out,
+    out,
     loads, flex, schur, coupling, inverse, match, corner, corner_pad,
     halo, near_coupling, near_corner,
-    perm, padded, wide_g, schur_g, select, near_inverse, inv_hi, inv_lo,
+    perm, padded, wide_g, schur_g, g_schur, g_schur_g, select, near_inverse, inv_hi, inv_lo,
     res, y_buf, free, z_buf, image,
     dense, recv1, part, chip, pair, recv2, total, rhs,
     local_sem, halo_send, halo_recv, near_send, near_recv,
@@ -128,7 +128,10 @@
     for f in range(4):
         o = OPPOSITE[f]
         remote(coupling.at[:, :, faces(f)], near_coupling.at[o], near_send.at[0], near_recv.at[0], near[f])
+    for f in range(4):
+        remote(corner_pad, near_corner.at[OPPOSITE[f]], near_send.at[1], near_recv.at[1], near[f])
     sent.append((near_coupling, near_send.at[0]))
+    sent.append((near_corner, near_send.at[1]))
 
     def send_out(step, f0, ref):
         for f in (f0, f0 + 1):
@@ -138,10 +141,6 @@
 
     send_out(0, 0, loads)
     send_out(0, 2, loads)
-    for f in range(4):
-        remote(corner_pad, near_corner.at[OPPOSITE[f]], near_send.at[1], near_recv.at[1], near[f])
-    sent.append((near_corner, near_send.at[1]))
-
     match_copy.wait()
     index = lax.broadcasted_iota(jnp.int32, (face, face), 0)
     for f in range(4):
@@ -168,13 +167,6 @@
         start = 16 * f + 16
         wide_g[start : start + 16, faces(f)] = both[:16].astype(BF16)
         wide_g[start + 128 : start + 144, faces(f)] = both[16:].astype(BF16)
-    schur_copy.wait()
-    for f in range(4):
-        both = dot_nt(schur[faces(f), :], wide_g[...])
-        hi, lo = split(0.5 * (both[:, :128] + both[:, 128:]))
-        schur_g[faces(f), 0:128] = hi
-        schur_g[faces(f), 128:256] = lo
-
     drain(near_corner, near_recv.at[1])
     lane = lax.broadcasted_iota(jnp.int32, (8, 128), 1)
     numbers = jnp.where(lane < corners, corner_pad[...], -1)
@@ -185,9 +177,15 @@
     turned = jnp.broadcast_to(numbers.astype(F32)[0:1, :], (128, 128)).T
     unknown = lax.broadcasted_iota(jnp.int32, (128, size), 1).astype(F32)
     select[...] = (turned[:, 0:1] == unknown).astype(BF16)
-
-    def start_coarse(it, both):
-        spread = dot(stacked(both[:, :128] + both[:, 128:]), select[...])
+    schur_copy.wait()
+    for f in range(4):
+        both = dot_nt(schur[faces(f), :], wide_g[...])
+        hi, lo = split(0.5 * (both[:, :128] + both[:, 128:]))
+        schur_g[faces(f), 0:128] = hi
+        schur_g[faces(f), 128:256] = lo
+
+    def start_coarse(it, mine):
+        spread = dot(stacked(mine), select[...])
         spread = spread[:load_cases] + spread[load_cases:]
         for t in range(n_sub):
             lg, h = t % 8, t // 8
@@ -237,28 +235,22 @@
         )
 
     def pick(both):
-        out = dot_nt(both, near_inverse[...])
+        out = dot(both, near_inverse[...])
         return out[:load_cases, :128] + out[:load_cases, 128:] + out[load_cases:, :128]
 
     def lowered(both):
-        low = dot_nt(both, inv_hi[...])
-        return low[:load_cases] + low[load_cases:] + dot_nt(both[:load_cases], inv_lo[...])
-
-    def spread_coarse(both, f):
-        out = dot(both, wide_g[0:128, faces(f)])
-        return out[:load_cases] + out[load_cases:] + dot(both[:load_cases], wide_g[128:256, faces(f)])
+        low = dot(both, inv_hi[...])
+        return low[:load_cases] + low[load_cases:] + dot(both[:load_cases], inv_lo[...])
+
+    def twice(both, matrix, cut):
+        out = dot(both, matrix[0:128, cut])
+        return out[:load_cases] + out[load_cases:] + dot(both[:load_cases], matrix[128:256, cut])
 
     def row_of(a, b):
         return jnp.sum(jnp.concatenate([a, b], axis=0).T, axis=0, keepdims=True)
 
     def tile(a):
         return jnp.concatenate([a] * (face // 128), axis=1)
-
-    def apply_schur(it, weighted):
-        for h in range(2):
-            cut = slice(half * h, half * h + half)
-            y_buf[it, :, cut] = dot(weighted, schur[:, cut])
-            send_out(2 * it + 1, 2 * h, y_buf.at[it])
 
     def start_flex(it):
         for f in (2, 3):
@@ -280,18 +272,17 @@
     for f in (0, 1):
         res[:, faces(f)] = loads[:, faces(f)] - neighbour(0, f)
     weighted = (0.5 * res[...]).astype(BF16)
-    start_coarse(0, both + dot(weighted[:, :half], schur_g[:half, :]))
-    apply_schur(0, weighted)
+    both = both + dot(weighted[:, :half], schur_g[:half, :])
+    start_coarse(0, both[:, :128] + both[:, 128:])
+    for h in range(2):
+        cut = slice(half * h, half * h + half)
+        y_buf[0, :, cut] = dot(weighted, schur[:, cut])
+        send_out(1, 2 * h, y_buf.at[0])
 
     inverse_copy.wait()
-    hi, lo = split(inverse[...])
+    hi, lo = split(inverse[...].T)
     inv_hi[...] = hi
     inv_lo[...] = lo
-    chosen_hi = dot_nt(select[...], inv_hi[...]).astype(BF16)
-    chosen_lo = dot_nt(select[...], inv_lo[...]).astype(BF16)
-    hi, lo = split(dot(chosen_hi, inv_hi[...]) + dot(chosen_lo, inv_hi[...]) + dot(chosen_hi, inv_lo[...]))
-    near_inverse[0:128, :] = hi
-    near_inverse[128:256, :] = lo
     flex_copy.wait()
 
     middle_coarse(0, plain)
@@ -299,18 +290,40 @@
     third_coarse(0, plain)
     finish_flex(0)
     rows = [row_of(lane_chunks(0.5 * res[...] * y_buf[0]), lane_chunks(z_buf[0] * free[0]))]
+
+    for f in range(4):
+        both = dot(wide_g[...], schur[:, faces(f)])
+        hi, lo = split(0.5 * (both[:128] + both[128:]))
+        g_schur[0:128, faces(f)] = hi
+        g_schur[128:256, faces(f)] = lo
+    both = dot(wide_g[...], schur_g[...])
+    hi, lo = split(0.5 * (both[:128, :128] + both[:128, 128:] + both[128:, :128]))
+    g_schur_g[0:128, :] = hi
+    g_schur_g[128:256, :] = lo
     flush()
     last_coarse(0, plain)
     for f in range(4):
         image[0, :, faces(f)] = free[0, :, faces(f)] - neighbour(2, f)
+    weighted = (0.5 * image[0]).astype(BF16)
+    y_buf[1] = dot(weighted, schur[...])
+    both = dot(weighted, schur_g[...])
+    mine = both[:, :128] + both[:, 128:]
+    chosen_hi = dot(select[...], inv_hi[...]).astype(BF16)
+    chosen_lo = dot(select[...], inv_lo[...]).astype(BF16)
+    both = dot_nt(inv_hi[...], jnp.concatenate([chosen_hi, chosen_lo], axis=0))
+    hi, lo = split(both[:, :128] + both[:, 128:] + dot_nt(inv_lo[...], chosen_hi))
+    near_inverse[:, 0:128] = hi
+    near_inverse[:, 128:256] = lo
     both_rhs = whole_coarse(0, plain)
     both = stacked(pick(both_rhs))
-    for f in range(4):
-        image[0, :, faces(f)] = image[0, :, faces(f)] + spread_coarse(both, f)
-
-    weighted = (0.5 * image[0]).astype(BF16)
-    apply_schur(1, weighted)
-    start_coarse(1, dot(weighted, schur_g[...]))
+
+    for h in range(2):
+        cut = slice(half * h, half * h + half)
+        y_buf[1, :, cut] = y_buf[1, :, cut] + twice(both, g_schur, cut)
+        send_out(3, 2 * h, y_buf.at[1])
+    start_coarse(1, mine + twice(both, g_schur_g, slice(0, 128)))
+    for f in range(4):
+        image[0, :, faces(f)] = image[0, :, faces(f)] + twice(both, wide_g, faces(f))
     low0 = lowered(both_rhs)
     rows.append(
         row_of(
@@ -322,12 +335,7 @@
     flush()
     start_flex(1)
     finish_flex(1)
-    rows.append(
-        row_of(
-            lane_chunks(z_buf[1] * free[0] + z_buf[0] * free[1]),
-            lane_chunks(z_buf[1] * free[1]),
-        )
-    )
+    rows.append(row_of(lane_chunks(2.0 * z_buf[1] * free[0]), lane_chunks(z_buf[1] * free[1])))
     for i, r in enumerate(rows):
         part[1, i : i + 1, width:] = r
     middle_coarse(1, wide)
@@ -361,11 +369,11 @@
     for f in range(4):
         sign = 1.0 if f % 2 else -1.0
         one, two = tile(sign * first), tile(sign * second)
-        mult_out[:, faces(f)] = one * z_buf[0, :, faces(f)] - two * z_buf[1, :, faces(f)]
-        res_out[:, faces(f)] = (
+        out[:, f, :] = one * z_buf[0, :, faces(f)] - two * z_buf[1, :, faces(f)]
+        out[:, f + 4, :] = (
             sign * res[:, faces(f)]
             - one * image[0, :, faces(f)]
-            + two * (image[1, :, faces(f)] + spread_coarse(both, f))
+            + two * (image[1, :, faces(f)] + twice(both, wide_g, faces(f)))
         )
 
 
@@ -385,8 +393,8 @@
             vmem(corner.shape, jnp.int32), vmem((8, 128), jnp.int32),
             vmem((5, 4, load_cases, face), F32), vmem((4, corners, 1, face), F32), vmem((4, 8, 128), jnp.int32),
             vmem((4, face, face), BF16), vmem((16, interface), F32), vmem((256, interface), BF16),
-            vmem((interface, 256), BF16), vmem((128, size), BF16),
-            vmem((256, size), BF16), vmem((size, size), BF16), vmem((size, size), BF16),
+            vmem((interface, 256), BF16), vmem((256, interface), BF16), vmem((256, 128), BF16), vmem((128, size), BF16),
+            vmem((size, 256), BF16), vmem((size, size), BF16), vmem((size, size), BF16),
             vmem(flat, F32), vmem((2,) + flat, F32), vmem((2,) + flat, F32), vmem((2,) + flat, F32),
             vmem((2,) + flat, F32),
             vmem((2, n_sub) + block, F32), vmem((2, n_sub - 1) + block, F32), vmem((2,) + wide, F32),
@@ -397,9 +405,9 @@
         ]
         out = pl.pallas_call(
             functools.partial(kernel, n_sub, n_grp),
-            out_shape=(jax.ShapeDtypeStruct(flat, F32), jax.ShapeDtypeStruct(flat, F32)),
+            out_shape=jax.ShapeDtypeStruct((load_cases, 8, face), F32),
             in_specs=[HBM] * 7,
-            out_specs=(VMEM, VMEM),
+            out_specs=VMEM,
             scratch_shapes=scratch,
             compiler_params=pltpu.CompilerParams(
                 collective_id=0, has_side_effects=True, vmem_limit_bytes=48 * 2**20
@@ -411,7 +419,8 @@
                 for x in (loads, flex, schur, coupling.transpose(0, 2, 1, 3), inverse, match, corner)
             )
         )
-        return tuple(x.reshape(1, 1, load_cases, 4, face) for x in out)
+        out = out[None, None]
+        return out[:, :, :, :4], out[:, :, :, 4:]
 
     split4 = P("sub", "grp", None, None)
     return jax.shard_map(

time: 58.4 us -> 56.2 us (0.962)
  Pallas kernels: 56 us -> 54.5 us
  local copies, waits for them, and re-layouts: 1.75 us -> 1 us
    reshape x2 -> x0, local copies, waits for them, and re-layouts: 1.75 us -> none  [shards(): return tuple((x.reshape(1, 1, load_cases, 4, face) for x in out))]
    pallas_call x1, Pallas kernels: 56 us -> 54.5 us  [shards(): pl.pallas_call(functools.partial(kernel, n_sub, n_grp), out_shape=jax.Sha...]
    slice x0 -> x1, local copies, waits for them, and re-layouts: none -> 1 us  [shards(): return (out[:, :, :, :4], out[:, :, :, 4:])]
where the time goes in v3:
time: 56.2 us; the launch traced here: 56.1 us
  Pallas kernels  54.5 us (97%)
  local copies, waits for them, and re-layouts  1 us (2%)
  between operations  0.64 us (1%)
    pallas_call x1, Pallas kernels, shards(): pl.pallas_call(functools.partial(kernel, n_sub, n_grp), out_shape=jax.Sha...  54.5 us

profile of v3, /device:TPU:1, one launch (start us, length us, event | category | flops | bytes accessed | tf_op | source)
XLA Modules:
  0.0 56.1 jit_solution(149315087793324233)
XLA Ops:
  0.6 54.5 %cg.1 = f32[64,8,384]{2,1,0:T(8,128)S(1)} custom-call(f32[1,1,64,1536]{3,2,1,0:T(8,128)} %loads_hbm.1, bf16[1,1,1536,1536]{3,2,1,0:T(8,128)(2,1)} %flex_hbm.1, bf16[1,1,1536,1536]{3,2,1,0:T(8,128)(2,1)} %schur_hbm.1, f32[1,12,1,1536]{3,2,1,0:T(1,128)} %bitcast.3, f32[768,768]{1,0:T(8,128)} %inverse_hbm.1, s32[1,1,4,384]{3,2,1,0:T(4,128)} %match_hbm.1, ...), custom_call_target="tpu_custom_call" | custom-call | tf_op jit(solution)/shard_map/cg/pallas_call | solution.py:406
  55.1 1.0 %fusion = (f32[1,1,64,4,384]{4,3,2,1,0:T(4,128)}, f32[1,1,64,4,384]{4,3,2,1,0:T(4,128)}) fusion(f32[1,1,64,8,384]{4,3,2,1,0:T(8,128)S(1)} %bitcast.2), kind=kLoop, calls=%fused_computation | loop fusion | bytes 1572864 | tf_op jit(solution)/shard_map/slice | solution.py:423

commit v4 on v3

--- a/solution.py
+++ b/solution.py
@@ -49,7 +49,7 @@
     out,
     loads, flex, schur, coupling, inverse, match, corner, corner_pad,
     halo, near_coupling, near_corner,
-    perm, padded, wide_g, schur_g, g_schur, g_schur_g, select, near_inverse, inv_hi, inv_lo,
+    perm, padded, wide_g, g_schur, g_schur_g, select, near_inverse, inv_hi, inv_lo,
     res, y_buf, free, z_buf, image,
     dense, recv1, part, chip, pair, recv2, total, rhs,
     local_sem, halo_send, halo_recv, near_send, near_recv,
@@ -152,6 +152,14 @@
         both = dot(stacked(halo[step, f]), perm[f])
         return both[:load_cases] + both[load_cases:]
 
+    def add_g_schur(first, last):
+        terms = jnp.concatenate([wide_g[first:last, :], wide_g[first + 128 : last + 128, :]], axis=0)
+        for f in range(4):
+            both = dot(terms, schur[:, faces(f)])
+            hi, lo = split(0.5 * (both[: last - first] + both[last - first :]))
+            g_schur[first:last, faces(f)] = hi
+            g_schur[first + 128 : last + 128, faces(f)] = lo
+
     wide_g[...] = jnp.zeros(wide_g.shape, BF16)
     padded[...] = jnp.zeros(padded.shape, F32)
     for k in range(corners):
@@ -159,6 +167,9 @@
     hi, lo = split(padded[...])
     wide_g[0:16, :] = hi
     wide_g[128:144, :] = lo
+    g_schur[...] = jnp.zeros(g_schur.shape, BF16)
+    schur_copy.wait()
+    add_g_schur(0, 16)
     drain(near_coupling, near_recv.at[0])
     for f in range(4):
         for k in range(corners):
@@ -177,12 +188,7 @@
     turned = jnp.broadcast_to(numbers.astype(F32)[0:1, :], (128, 128)).T
     unknown = lax.broadcasted_iota(jnp.int32, (128, size), 1).astype(F32)
     select[...] = (turned[:, 0:1] == unknown).astype(BF16)
-    schur_copy.wait()
-    for f in range(4):
-        both = dot_nt(schur[faces(f), :], wide_g[...])
-        hi, lo = split(0.5 * (both[:, :128] + both[:, 128:]))
-        schur_g[faces(f), 0:128] = hi
-        schur_g[faces(f), 128:256] = lo
+    add_g_schur(16, 80)
 
     def start_coarse(it, mine):
         spread = dot(stacked(mine), select[...])
@@ -268,11 +274,11 @@
 
     for f in (2, 3):
         res[:, faces(f)] = loads[:, faces(f)] - neighbour(0, f)
-    both = dot((0.5 * res[:, half:]).astype(BF16), schur_g[half:, :])
+    both = dot_nt((0.5 * res[:, half:]).astype(BF16), g_schur[:, half:])
     for f in (0, 1):
         res[:, faces(f)] = loads[:, faces(f)] - neighbour(0, f)
     weighted = (0.5 * res[...]).astype(BF16)
-    both = both + dot(weighted[:, :half], schur_g[:half, :])
+    both = both + dot_nt(weighted[:, :half], g_schur[:, :half])
     start_coarse(0, both[:, :128] + both[:, 128:])
     for h in range(2):
         cut = slice(half * h, half * h + half)
@@ -291,12 +297,7 @@
     finish_flex(0)
     rows = [row_of(lane_chunks(0.5 * res[...] * y_buf[0]), lane_chunks(z_buf[0] * free[0]))]
 
-    for f in range(4):
-        both = dot(wide_g[...], schur[:, faces(f)])
-        hi, lo = split(0.5 * (both[:128] + both[128:]))
-        g_schur[0:128, faces(f)] = hi
-        g_schur[128:256, faces(f)] = lo
-    both = dot(wide_g[...], schur_g[...])
+    both = dot_nt(wide_g[...], g_schur[...])
     hi, lo = split(0.5 * (both[:128, :128] + both[:128, 128:] + both[128:, :128]))
     g_schur_g[0:128, :] = hi
     g_schur_g[128:256, :] = lo
@@ -306,7 +307,7 @@
         image[0, :, faces(f)] = free[0, :, faces(f)] - neighbour(2, f)
     weighted = (0.5 * image[0]).astype(BF16)
     y_buf[1] = dot(weighted, schur[...])
-    both = dot(weighted, schur_g[...])
+    both = dot_nt(weighted, g_schur[...])
     mine = both[:, :128] + both[:, 128:]
     chosen_hi = dot(select[...], inv_hi[...]).astype(BF16)
     chosen_lo = dot(select[...], inv_lo[...]).astype(BF16)
@@ -393,7 +394,7 @@
             vmem(corner.shape, jnp.int32), vmem((8, 128), jnp.int32),
             vmem((5, 4, load_cases, face), F32), vmem((4, corners, 1, face), F32), vmem((4, 8, 128), jnp.int32),
             vmem((4, face, face), BF16), vmem((16, interface), F32), vmem((256, interface), BF16),
-            vmem((interface, 256), BF16), vmem((256, interface), BF16), vmem((256, 128), BF16), vmem((128, size), BF16),
+            vmem((256, interface), BF16), vmem((256, 128), BF16), vmem((128, size), BF16),
             vmem((size, 256), BF16), vmem((size, size), BF16), vmem((size, size), BF16),
             vmem(flat, F32), vmem((2,) + flat, F32), vmem((2,) + flat, F32), vmem((2,) + flat, F32),
             vmem((2,) + flat, F32),

time: 56.2 us -> 56.2 us (level)
  no operation moved by 1% of the time
where the time goes in v4:
time: 56.2 us; the launch traced here: 56.1 us
  Pallas kernels  54.5 us (97%)
  local copies, waits for them, and re-layouts  1 us (2%)
  between operations  0.64 us (1%)
    pallas_call x1, Pallas kernels, shards(): pl.pallas_call(functools.partial(kernel, n_sub, n_grp), out_shape=jax.Sha...  54.5 us

profile of v4, /device:TPU:1, one launch (start us, length us, event | category | flops | bytes accessed | tf_op | source)
XLA Modules:
  0.0 56.1 jit_solution(17222378585823640958)
XLA Ops:
  0.6 54.5 %cg.1 = f32[64,8,384]{2,1,0:T(8,128)S(1)} custom-call(f32[1,1,64,1536]{3,2,1,0:T(8,128)} %loads_hbm.1, bf16[1,1,1536,1536]{3,2,1,0:T(8,128)(2,1)} %flex_hbm.1, bf16[1,1,1536,1536]{3,2,1,0:T(8,128)(2,1)} %schur_hbm.1, f32[1,12,1,1536]{3,2,1,0:T(1,128)} %bitcast.3, f32[768,768]{1,0:T(8,128)} %inverse_hbm.1, s32[1,1,4,384]{3,2,1,0:T(4,128)} %match_hbm.1, ...), custom_call_target="tpu_custom_call" | custom-call | tf_op jit(solution)/shard_map/cg/pallas_call | solution.py:407
  55.2 1.0 %fusion = (f32[1,1,64,4,384]{4,3,2,1,0:T(4,128)}, f32[1,1,64,4,384]{4,3,2,1,0:T(4,128)}) fusion(f32[1,1,64,8,384]{4,3,2,1,0:T(8,128)S(1)} %bitcast.2), kind=kLoop, calls=%fused_computation | loop fusion | bytes 1572864 | tf_op jit(solution)/shard_map/slice | solution.py:424
